TPU v7x, 256 devices: a whole 4x4x8 slice. The times are simulated.
256 devices in a mesh: ctx: 64 (over z, x, core), ch: 4 (over y).
Axes of the slice: x: 4, y: 4, z: 8, core: 2. Of those that a mesh axis runs over, the one named last changes fastest.
Arguments:
- streams: bfloat16 [3, 16384, 4096], P(None, 'ctx', 'ch'), may hold values from -6 to 6
- residual_in: bfloat16 [16384, 4096], P('ctx', 'ch'), may hold values from -6 to 6
- short_filter: float32 [3, 7, 4096], replicated, may hold values from -2 to 2
- medium_filter: bfloat16 [128, 4096], P(None, 'ch'), may hold values from -4 to 4
- skip_gain: float32 [4096], P('ch'), may hold values from -4 to 4
- w_out: bfloat16 [4096, 4096], P(('ch', 'ctx')), may hold values from -0.375 to 0.375
Outputs:
- block_out: bfloat16 [16384, 4096], P('ctx', 'ch')
All inputs are finite; a program needn't handle non-finite values.
Results may differ from a plain program's by a relative error of at most 0.019.
Values may be sent and summed in bfloat16 or wider, within the bound.
A program may use at most 256 MiB of HBM per device.

v0:
```python
import functools

import jax
import jax.numpy as jnp
import numpy as np
from jax import lax
from jax.experimental import pallas as pl
from jax.experimental.pallas import tpu as pltpu
from jax.sharding import PartitionSpec as P

MESH = pl.DeviceIdType.MESH
NZ, NX, NC, NY = 8, 4, 2, 4
TOK = 256
CH = 1024
FILT = 128
SHORT = 7
ROWS = 16
WIN = FILT + TOK
HALF = WIN // 2
BLK = 256
CUT = 640
UP = 2
EDGE = FILT + ROWS
N_COPIES = 128


def transforms():
    freq = np.arange(HALF) + 0.5
    angle = 2 * np.pi * np.outer(freq, np.arange(WIN)) / WIN
    forward = np.concatenate([np.cos(angle), -np.sin(angle)], axis=0)
    inverse = forward.T[FILT:] * (2.0 / WIN)
    return forward, inverse


ORDER = (
    "s1", "em1u", "s3", "s2", "rim", "ex0u", "em1d", "sh1", "rimp", "sh0", "m1d", "m1u", "x0u", "o0", "spec", "ex0d",
    "fix", "x0d", "o2", "o1", "m2d", "x1u", "m2u", "x1d", "c1", "g1d", "g1u", "xx0u", "xx0d", "c0", "x7d", "g0d",
    "n1u", "n1d", "x7u", "g0u", "o3", "c3", "m3d", "xx1u", "m3u", "x2u", "x6d", "xx1d", "c2", "f1u", "g3u", "f1d",
    "x6u", "g2d", "xx7d", "n2u", "x2d", "g2u", "g3d", "h1d", "xx7u", "n2d", "m4u", "x3u", "x5d", "h0d", "m4d", "x3d",
    "xx6d", "f2u", "h1u", "f2d", "x5u", "xx6u", "xx2u", "t0", "h0u", "n3u", "n3d", "xx2d", "t7", "t1", "h2d", "x4d",
    "h2u", "x4u", "h3u", "h3d", "f3u", "f3d", "xx3d", "xx3u", "xx5u", "xx5d", "t6", "n4u", "n4d", "f4u", "t2",
    "xx4u", "xx4d", "f4d", "p0", "t3", "p7", "t5", "p1", "p6", "t4x", "t4z", "p2", "p5", "p3", "p4",
)
N_LOCAL = 9


def kernel(
    streams, residual, short, medium, skip, w_out, fwd_a, fwd_b, inv,
    out,
    sx, taps, med, gain, fwd_av, fwd_bv, inv_v, res, prod, query, spec, freq, wbuf, gbuf, acc,
    send, recv, local,
):
    me, y = lax.axis_index("ctx"), lax.axis_index("ch")
    c = lax.rem(me, NC)
    x = lax.rem(me // NC, NX)
    z = me // (NC * NX)

    def at(zz, xx, cc):
        return (lax.rem(zz + NZ, NZ) * NX + lax.rem(xx + NX, NX)) * NC + cc

    def ymod(v):
        return lax.rem(v + NY, NY)

    n_ctx = NZ * NX * NC
    z_to = {"u": (at(z + 1, x, c), y), "d": (at(z - 1, x, c), y)}
    x_to = {"u": (at(z, x + 1, c), y), "d": (at(z, x - 1, c), y)}
    y_to = {"u": (me, ymod(y + 1)), "d": (me, ymod(y - 1))}
    twin, y_far = (at(z, x, 1 - c), y), (me, ymod(y + 2))
    after, before = (lax.rem(me + 1, n_ctx), y), (lax.rem(me + n_ctx - 1, n_ctx), y)

    def owned(group):
        return pl.ds(pl.multiple_of(group * CH, CH), CH)

    loads = {}
    for i, (name, src, dst) in enumerate(
        (
            ("streams", streams, sx.at[:, pl.ds(ROWS, TOK), :]),
            ("short", short.at[:, :, owned(y)], taps),
            ("w_out", w_out.at[:, owned(y)], wbuf.at[0, c, 0, 0]),
            ("medium", medium, med),
            ("fwd_a", fwd_a, fwd_av),
            ("fwd_b", fwd_b, fwd_bv),
            ("skip", skip, gain),
            ("inv", inv, inv_v),
            ("residual", residual, res),
        )
    ):
        loads[name] = pltpu.make_async_copy(src, dst, local.at[i])
        loads[name].start()

    def loaded(*wanted):
        for name in wanted:
            if name in loads:
                loads.pop(name).wait()

    barrier = pltpu.get_barrier_semaphore()
    friends = (*z_to.values(), *x_to.values(), *y_to.values(), y_far, twin, after, before)
    for friend in friends:
        pl.semaphore_signal(barrier, inc=1, device_id=friend, device_id_type=MESH)
    pl.semaphore_wait(barrier, len(friends))

    moves = {}
    whole, x_cols, z_cols = pl.ds(0, CH), pl.ds(0, CUT), pl.ds(CUT, CH - CUT)
    every, rest = pl.ds(0, NY), pl.ds(1, NY - 1)
    half_z = {"u": pl.ds(0, 2), "d": pl.ds(2, 2)}
    half_x = {"u": pl.ds(0, UP), "d": pl.ds(UP, NY - UP)}
    own, near, far = pl.ds(0, 1), pl.ds(1, 2), pl.ds(3, 1)

    for k, device in ((1, y_to["u"]), (2, y_far), (3, y_to["d"])):
        moves[f"s{k}"] = (
            w_out.at[:, owned(ymod(y + k))], wbuf.at[0, c, 0, NY - k], device, ()
        )
    moves["rim"] = (streams.at[:, pl.ds(TOK - ROWS, ROWS), :], sx.at[:, pl.ds(0, ROWS), :], after, ())
    moves["rimp"] = (prod.at[pl.ds(TOK, FILT), :], prod.at[pl.ds(0, FILT), :], after, ("sh1",))

    def along_z(name, step, way, slots, groups, cols, needs):
        src = (1 - step) % NZ if way == "u" else step - 1
        dst = (src - 1) % NZ if way == "u" else src + 1
        moves[name] = (
            wbuf.at[src, c, slots, groups, :, cols],
            wbuf.at[dst, c, slots, groups, :, cols],
            z_to[way],
            needs,
        )

    def along_x(name, dz, way, src, dst, groups, cols, needs):
        moves[name] = (
            wbuf.at[dz, c, src, groups, :, cols], wbuf.at[dz, c, dst, groups, :, cols], x_to[way], needs
        )

    spread = ("s1", "s2", "s3")
    begun = ("x0u", "x0d", "ex0u", "ex0d")
    from_z = {0: begun, 4: ("m4u", "m4d")}
    for way in "ud":
        near_slot = 2 if way == "u" else 1
        mine = w_out.at[:, owned(y)]
        moves["em1" + way] = (mine, wbuf.at[7 if way == "u" else 1, c, 0, 0], z_to[way], ())
        along_z("m1" + way, 1, way, own, rest, whole, spread)
        moves["ex0" + way] = (mine, wbuf.at[0, c, near_slot, 0], x_to[way], ())
        along_x("x0" + way, 0, way, 0, near_slot, rest, whole, spread)
        for step in range(2, NZ // 2 + 1):
            last = step == NZ // 2
            groups = half_z[way] if last else every
            needs = ("m1" + way, "em1" + way) if step == 2 else (f"m{step - 1}{way}",)
            along_z(f"m{step}{way}", step, way, own, groups, whole, needs)
            along_z(f"n{step}{way}", step, way, near, groups, z_cols, (f"n{step - 1}{way}",))
            along_z(f"f{step}{way}", step, way, far, groups, z_cols, (f"f{step - 1}{way}",))
        along_z("n1" + way, 1, way, near, every, z_cols, begun)
        along_z("f1" + way, 1, way, far, every, z_cols, ("xx0u", "xx0d"))
        for dz in range(NZ):
            if dz not in from_z:
                step = min(dz, NZ - dz)
                ways = "d" if dz < NZ // 2 else "u"
                from_z[dz] = tuple(f"{kind}{step}{ways}" for kind in ("m", "em")[: 2 if step == 1 else 1])
            cols = x_cols if dz else whole
            if dz:
                along_x(f"x{dz}{way}", dz, way, 0, near_slot, every, cols, from_z[dz])
            needs = (f"x{dz}{way}",) if dz else ("x0" + way, "ex0" + way)
            along_x(f"xx{dz}{way}", dz, way, near_slot, 3, half_x[way], cols, needs)
        for b in range(CH // BLK):
            per = BLK // 128
            chunk = pl.ds(b * per, per)
            half = pl.ds(b * per + (0 if way == "u" else per // 2), per // 2)
            group = 3 if way == "u" else 1
            moves[f"g{b}{way}"] = (gbuf.at[0, chunk], gbuf.at[group, chunk], y_to[way], (f"c{b}",))
            moves[f"h{b}{way}"] = (gbuf.at[group, half], gbuf.at[2, half], y_to[way], (f"g{b}{way}",))
    for dz in range(NZ):
        by_x = from_z[dz] + tuple(f"{kind}{dz}{way}" for kind in ("x", "xx") for way in "ud")
        step = min(dz, NZ - dz)
        ways = "ud" if dz == NZ // 2 else "d" if dz < NZ // 2 else "u"
        by_z = tuple(f"{kind}{step}{way}" for kind in ("n", "f") for way in ways) if dz else ()
        if dz == 0:
            by_x = ("own",) + spread + by_x
        if dz == NZ // 2:
            for name, cols, needs in (("t4x", x_cols, by_x), ("t4z", z_cols, by_z + from_z[dz])):
                part = wbuf.at[dz, c, :, :, :, cols]
                moves[name] = (part, part, twin, needs)
        else:
            moves[f"t{dz}"] = (wbuf.at[dz, c], wbuf.at[dz, c], twin, by_x + by_z)

    def short_rows(start, rows):
        def lane_block(b, carry):
            lanes = pl.ds(pl.multiple_of(b * 128, 128), 128)
            done = []
            for s in range(3):
                window = sx[s, pl.ds(start, rows + ROWS), lanes].astype(jnp.float32)
                total = None
                for j in range(SHORT):
                    term = taps[s, j : j + 1, lanes] * window[ROWS - j : ROWS - j + rows]
                    total = term if total is None else total + term
                done.append(total)
            query[pl.ds(start, rows), lanes] = done[0]
            prod[pl.ds(FILT + start, rows), lanes] = (done[1] * done[2]).astype(jnp.bfloat16)
            return carry

        lax.fori_loop(0, CH // 128, lane_block, 0)

    def short_last():
        loaded("streams", "short")
        short_rows(FILT, FILT)

    def short_first():
        short_rows(ROWS, FILT - ROWS)

    def short_edge():
        @pl.when(me == 0)
        def _():
            sx[:, 0:ROWS, :] = jnp.zeros((3, ROWS, CH), jnp.bfloat16)

        short_rows(0, ROWS)

    def filter_spectrum():
        loaded("medium", "fwd_a")

        def body(b, carry):
            lanes = pl.ds(pl.multiple_of(b * BLK, BLK), BLK)
            spec[:, lanes] = jnp.dot(
                fwd_av[:, 0:FILT], med[:, lanes], preferred_element_type=jnp.float32
            )
            return carry

        lax.fori_loop(0, CH // BLK, body, 0)

    def own_spectrum(b):
        loaded("fwd_b")
        lanes = pl.ds(b * BLK, BLK)
        freq[:, lanes] = jnp.dot(
            fwd_bv[...], prod[EDGE:WIN, lanes], preferred_element_type=jnp.float32
        )

    edge_ready = []

    def conv_block(b):
        loaded("skip", "inv")
        if not edge_ready:
            edge_ready.append(b)

            @pl.when(me == 0)
            def _():
                prod[0:FILT, :] = jnp.zeros((FILT, CH), jnp.bfloat16)

        lanes = pl.ds(b * BLK, BLK)
        total = freq[:, lanes] + jnp.dot(
            fwd_av[...], prod[0:EDGE, lanes], preferred_element_type=jnp.float32
        )
        fr, fi = total[:HALF], total[HALF:]
        hr, hi = spec[0:HALF, lanes], spec[HALF:WIN, lanes]
        both = jnp.concatenate([fr * hr - fi * hi, fr * hi + fi * hr], axis=0).astype(jnp.bfloat16)
        mixed = jnp.dot(inv_v[...], both, preferred_element_type=jnp.float32)
        direct = gain[0:1, lanes] * prod[pl.ds(FILT, TOK), lanes].astype(jnp.float32)
        gated = (query[:, lanes] * (mixed + direct)).astype(jnp.bfloat16)
        for part in range(BLK // 128):
            gbuf[0, b * (BLK // 128) + part] = gated[:, part * 128 : (part + 1) * 128]

    projected = []

    def project(dz):
        loaded("residual")
        begin, end = not projected, len(projected) == NZ - 1
        projected.append(dz)
        plane = lax.rem(z + dz, NZ)

        def body(n, carry):
            cols = pl.ds(pl.multiple_of(n * 256, 256), 256)
            total = res[:, cols].astype(jnp.float32) if begin else acc[:, cols]
            left = jnp.concatenate([gbuf[g, plane] for g in range(NY)], axis=1)
            pieces = []
            for g in range(NY):
                for xx in range(NX):
                    dx = lax.rem(xx - x + NX, NX)
                    slot = dx + dx // 2 - 2 * (dx // 3)
                    pieces += [wbuf[dz, cc, slot, g, :, cols] for cc in range(NC)]
            right = jnp.concatenate(pieces, axis=0)
            total = total + jnp.dot(left, right, preferred_element_type=jnp.float32)
            if end:
                out[:, cols] = total.astype(jnp.bfloat16)
            else:
                acc[:, cols] = total
            return carry

        lax.fori_loop(0, CH // 256, body, 0)

    tasks = {
        "sh1": (short_last, ()),
        "sh0": (short_first, ()),
        "spec": (filter_spectrum, ()),
        "fix": (short_edge, ("rim", "sh1")),
    }
    for b in range(CH // BLK):
        tasks[f"o{b}"] = (functools.partial(own_spectrum, b), ("sh1", "sh0"))
        tasks[f"c{b}"] = (functools.partial(conv_block, b), ("rimp", "fix", "spec", f"o{b}"))
    gated_all = tuple(f"{kind}{b}{way}" for kind in "gh" for b in range(CH // BLK) for way in "ud")
    for dz in range(NZ):
        twins = (f"t{dz}",) if dz != NZ // 2 else ("t4x", "t4z")
        tasks[f"p{dz}"] = (functools.partial(project, dz), twins + gated_all)

    copies, seen, ran = {}, set(), set()

    def await_all(needs):
        for name in needs:
            if name == "own":
                loaded("w_out")
            elif name in tasks:
                assert name in ran
            elif name not in seen:
                seen.add(name)
                copies[name].wait_recv()

    assert sorted(ORDER) == sorted([*moves, *tasks])
    for name in ORDER:
        if name in tasks:
            task, needs = tasks[name]
            await_all(needs)
            task()
            ran.add(name)
            continue
        src, dst, device, needs = moves[name]
        await_all(needs)
        i = len(copies)
        copies[name] = pltpu.make_async_remote_copy(
            src_ref=src,
            dst_ref=dst,
            send_sem=send.at[i],
            recv_sem=recv.at[i],
            device_id=device,
            device_id_type=MESH,
        )
        copies[name].start()
    await_all(copies)
    for copy in copies.values():
        copy.wait_send()


def on_device(streams, residual_in, short_filter, medium_filter, skip_gain, w_out):
    forward, inverse = transforms()
    fwd_a = jnp.asarray(forward[:, :EDGE].astype(np.float32), dtype=jnp.bfloat16)
    fwd_b = jnp.asarray(forward[:, EDGE:].astype(np.float32), dtype=jnp.bfloat16)
    inv = jnp.asarray(inverse.astype(np.float32), dtype=jnp.bfloat16)
    hbm = pl.BlockSpec(memory_space=pl.ANY)
    bf16, f32 = jnp.bfloat16, jnp.float32
    return pl.pallas_call(
        kernel,
        out_shape=jax.ShapeDtypeStruct((TOK, CH), bf16),
        in_specs=[hbm] * 9,
        out_specs=pl.BlockSpec(memory_space=pltpu.VMEM),
        scratch_shapes=[
            pltpu.VMEM((3, ROWS + TOK, CH), bf16),
            pltpu.VMEM((3, SHORT, CH), f32),
            pltpu.VMEM((FILT, CH), bf16),
            pltpu.VMEM((1, CH), f32),
            pltpu.VMEM((WIN, EDGE), bf16),
            pltpu.VMEM((WIN, WIN - EDGE), bf16),
            pltpu.VMEM((TOK, WIN), bf16),
            pltpu.VMEM((TOK, CH), bf16),
            pltpu.VMEM((WIN, CH), bf16),
            pltpu.VMEM((TOK, CH), f32),
            pltpu.VMEM((WIN, CH), f32),
            pltpu.VMEM((WIN, CH), f32),
            pltpu.VMEM((NZ, NC, NX, NY, ROWS, CH), bf16),
            pltpu.VMEM((NY, CH // 128, TOK, 128), bf16),
            pltpu.VMEM((TOK, CH), f32),
            pltpu.SemaphoreType.DMA((N_COPIES,)),
            pltpu.SemaphoreType.DMA((N_COPIES,)),
            pltpu.SemaphoreType.DMA((N_LOCAL,)),
        ],
        compiler_params=pltpu.CompilerParams(
            collective_id=0, has_side_effects=True, vmem_limit_bytes=63 * 1024 * 1024
        ),
    )(streams, residual_in, short_filter, medium_filter, skip_gain.reshape(1, CH), w_out, fwd_a, fwd_b, inv)


def solution(mesh):
    placed = (
        P(None, "ctx", "ch"),
        P("ctx", "ch"),
        P(),
        P(None, "ch"),
        P("ch"),
        P(("ch", "ctx"), None),
    )
    return jax.shard_map(
        on_device, mesh=mesh, in_specs=placed, out_specs=P("ctx", "ch"), check_vma=False
    )
```

profile of v0, /device:TPU:1, one launch (start us, length us, event | category | flops | bytes accessed | tf_op | source)
XLA Modules:
  0.0 50.9 jit_solution(18279632962532708456)
XLA Ops:
  0.0 49.1 %shard_map.91 = bf16[256,1024]{1,0:T(8,128)(2,1)} custom-call(bf16[3,256,1024]{2,1,0:T(8,128)(2,1)} %streams.1, bf16[256,1024]{1,0:T(8,128)(2,1)} %residual.1, f32[3,7,4096]{2,1,0:T(8,128)} %short.1, bf16[128,1024]{1,0:T(8,128)(2,1)} %medium.1, f32[1,1024]{1,0:T(1,128)} %bitcast.1, bf16[16,4096]{1,0:T(8,128)(2,1)} %w_out.1, ...), custom_call_target="tpu_custom_call" | custom-call | tf_op jit(solution)/shard_map/pallas_call | solution.py:341
  49.1 1.9 %copy.11 = bf16[256,1024]{1,0:T(8,128)(2,1)} copy(bf16[256,1024]{1,0:T(8,128)(2,1)} %shard_map.91) | data formatting | bytes 1048576
where the time goes:
time: 51.1 us; the launch traced here: 50.9 us
  Pallas kernels  49.1 us (96%)
  local copies, waits for them, and re-layouts  1.87 us (4%)
    pallas_call x1, Pallas kernels, on_device(): pl.pallas_call(kernel, out_shape=jax.ShapeDtypeStruct((TOK, CH), bf16), i...  49.1 us
    unnamed x1, local copies, waits for them, and re-layouts  1.87 us

commit v1 on v0

--- a/solution.py
+++ b/solution.py
@@ -20,6 +20,7 @@
 BLK = 256
 CUT = 640
 UP = 2
+LESS_UP = ()
 EDGE = FILT + ROWS
 N_COPIES = 128
 
@@ -33,13 +34,13 @@
 
 
 ORDER = (
-    "s1", "em1u", "s3", "s2", "rim", "ex0u", "em1d", "sh1", "rimp", "sh0", "m1d", "m1u", "x0u", "o0", "spec", "ex0d",
-    "fix", "x0d", "o2", "o1", "m2d", "x1u", "m2u", "x1d", "c1", "g1d", "g1u", "xx0u", "xx0d", "c0", "x7d", "g0d",
-    "n1u", "n1d", "x7u", "g0u", "o3", "c3", "m3d", "xx1u", "m3u", "x2u", "x6d", "xx1d", "c2", "f1u", "g3u", "f1d",
-    "x6u", "g2d", "xx7d", "n2u", "x2d", "g2u", "g3d", "h1d", "xx7u", "n2d", "m4u", "x3u", "x5d", "h0d", "m4d", "x3d",
-    "xx6d", "f2u", "h1u", "f2d", "x5u", "xx6u", "xx2u", "t0", "h0u", "n3u", "n3d", "xx2d", "t7", "t1", "h2d", "x4d",
-    "h2u", "x4u", "h3u", "h3d", "f3u", "f3d", "xx3d", "xx3u", "xx5u", "xx5d", "t6", "n4u", "n4d", "f4u", "t2",
-    "xx4u", "xx4d", "f4d", "p0", "t3", "p7", "t5", "p1", "p6", "t4x", "t4z", "p2", "p5", "p3", "p4",
+    "s1", "rim", "em1d", "s3", "s2", "em1u", "sh1", "rimp", "m1u", "x0d", "m1d", "ex0u", "sh0", "ex0d", "x0u", "o2",
+    "fix", "spec", "o0", "o1", "m2u", "x1d", "x7u", "m2d", "x1u", "x7d", "c0", "xx0d", "g0d", "n1u", "xx0u", "n1d",
+    "g0u", "c1", "c2", "g2u", "xx1d", "x6u", "x6d", "g2d", "m3d", "g1d", "m3u", "xx7u", "o3", "x2d", "h0u", "xx1u",
+    "g1u", "xx7d", "f1d", "f1u", "x2u", "c3", "n2d", "n2u", "m4d", "m4u", "xx6u", "g3d", "x3d", "t0", "xx6d", "x5u",
+    "g3u", "f2d", "f2u", "h2d", "h2u", "x3u", "x5d", "h0d", "n3d", "n3u", "h1d", "x4u", "x4d", "xx2u", "xx2d", "h3d",
+    "t7", "h1u", "f3d", "f3u", "xx3u", "t6", "t1", "xx5u", "xx3d", "xx5d", "h3u", "n4u", "n4d", "xx4u", "xx4d",
+    "f4u", "f4d", "t2", "t3", "p0", "t5", "p7", "p1", "t4x", "t4z", "p6", "p2", "p5", "p3", "p4",
 )
 N_LOCAL = 9
 
@@ -103,7 +104,11 @@
     whole, x_cols, z_cols = pl.ds(0, CH), pl.ds(0, CUT), pl.ds(CUT, CH - CUT)
     every, rest = pl.ds(0, NY), pl.ds(1, NY - 1)
     half_z = {"u": pl.ds(0, 2), "d": pl.ds(2, 2)}
-    half_x = {"u": pl.ds(0, UP), "d": pl.ds(UP, NY - UP)}
+
+    def half_x(dz, way):
+        groups = UP - 1 if dz in LESS_UP else UP
+        return pl.ds(0, groups) if way == "u" else pl.ds(groups, NY - groups)
+
     own, near, far = pl.ds(0, 1), pl.ds(1, 2), pl.ds(3, 1)
 
     for k, device in ((1, y_to["u"]), (2, y_far), (3, y_to["d"])):
@@ -156,7 +161,7 @@
             if dz:
                 along_x(f"x{dz}{way}", dz, way, 0, near_slot, every, cols, from_z[dz])
             needs = (f"x{dz}{way}",) if dz else ("x0" + way, "ex0" + way)
-            along_x(f"xx{dz}{way}", dz, way, near_slot, 3, half_x[way], cols, needs)
+            along_x(f"xx{dz}{way}", dz, way, near_slot, 3, half_x(dz, way), cols, needs)
         for b in range(CH // BLK):
             per = BLK // 128
             chunk = pl.ds(b * per, per)
@@ -212,14 +217,11 @@
     def filter_spectrum():
         loaded("medium", "fwd_a")
 
-        def body(b, carry):
-            lanes = pl.ds(pl.multiple_of(b * BLK, BLK), BLK)
+        for b in range(CH // BLK):
+            lanes = pl.ds(b * BLK, BLK)
             spec[:, lanes] = jnp.dot(
                 fwd_av[:, 0:FILT], med[:, lanes], preferred_element_type=jnp.float32
             )
-            return carry
-
-        lax.fori_loop(0, CH // BLK, body, 0)
 
     def own_spectrum(b):
         loaded("fwd_b")
@@ -260,10 +262,9 @@
         projected.append(dz)
         plane = lax.rem(z + dz, NZ)
 
-        def body(n, carry):
-            cols = pl.ds(pl.multiple_of(n * 256, 256), 256)
-            total = res[:, cols].astype(jnp.float32) if begin else acc[:, cols]
-            left = jnp.concatenate([gbuf[g, plane] for g in range(NY)], axis=1)
+        left = jnp.concatenate([gbuf[g, plane] for g in range(NY)], axis=1)
+        for n in range(CH // BLK):
+            cols = pl.ds(n * BLK, BLK)
             pieces = []
             for g in range(NY):
                 for xx in range(NX):
@@ -271,14 +272,12 @@
                     slot = dx + dx // 2 - 2 * (dx // 3)
                     pieces += [wbuf[dz, cc, slot, g, :, cols] for cc in range(NC)]
             right = jnp.concatenate(pieces, axis=0)
+            total = res[:, cols].astype(jnp.float32) if begin else acc[:, cols]
             total = total + jnp.dot(left, right, preferred_element_type=jnp.float32)
             if end:
                 out[:, cols] = total.astype(jnp.bfloat16)
             else:
                 acc[:, cols] = total
-            return carry
-
-        lax.fori_loop(0, CH // 256, body, 0)
 
     tasks = {
         "sh1": (short_last, ()),

time: 51.1 us -> 49.6 us (0.971)
  Pallas kernels: 49.1 us -> 47.6 us
    pallas_call x1, Pallas kernels: 49.1 us -> 47.6 us  [on_device(): pl.pallas_call(kernel, out_shape=jax.ShapeDtypeStruct((TOK, CH), bf16), i...]
where the time goes in v1:
time: 49.6 us; the launch traced here: 49.4 us
  Pallas kernels  47.6 us (96%)
  local copies, waits for them, and re-layouts  1.87 us (4%)
    pallas_call x1, Pallas kernels, on_device(): pl.pallas_call(kernel, out_shape=jax.ShapeDtypeStruct((TOK, CH), bf16), i...  47.6 us
    unnamed x1, local copies, waits for them, and re-layouts  1.87 us

profile of v1, /device:TPU:1, one launch (start us, length us, event | category | flops | bytes accessed | tf_op | source)
XLA Modules:
  0.0 49.4 jit_solution(8358533288636203907)
XLA Ops:
  0.0 47.6 %shard_map.91 = bf16[256,1024]{1,0:T(8,128)(2,1)} custom-call(bf16[3,256,1024]{2,1,0:T(8,128)(2,1)} %streams.1, bf16[256,1024]{1,0:T(8,128)(2,1)} %residual.1, f32[3,7,4096]{2,1,0:T(8,128)} %short.1, bf16[128,1024]{1,0:T(8,128)(2,1)} %medium.1, f32[1,1024]{1,0:T(1,128)} %bitcast.1, bf16[16,4096]{1,0:T(8,128)(2,1)} %w_out.1, ...), custom_call_target="tpu_custom_call" | custom-call | tf_op jit(solution)/shard_map/pallas_call | solution.py:340
  47.6 1.9 %copy.11 = bf16[256,1024]{1,0:T(8,128)(2,1)} copy(bf16[256,1024]{1,0:T(8,128)(2,1)} %shard_map.91) | data formatting | bytes 1048576

commit v2 on v1

--- a/solution.py
+++ b/solution.py
@@ -34,21 +34,21 @@
 
 
 ORDER = (
-    "s1", "rim", "em1d", "s3", "s2", "em1u", "sh1", "rimp", "m1u", "x0d", "m1d", "ex0u", "sh0", "ex0d", "x0u", "o2",
-    "fix", "spec", "o0", "o1", "m2u", "x1d", "x7u", "m2d", "x1u", "x7d", "c0", "xx0d", "g0d", "n1u", "xx0u", "n1d",
-    "g0u", "c1", "c2", "g2u", "xx1d", "x6u", "x6d", "g2d", "m3d", "g1d", "m3u", "xx7u", "o3", "x2d", "h0u", "xx1u",
-    "g1u", "xx7d", "f1d", "f1u", "x2u", "c3", "n2d", "n2u", "m4d", "m4u", "xx6u", "g3d", "x3d", "t0", "xx6d", "x5u",
-    "g3u", "f2d", "f2u", "h2d", "h2u", "x3u", "x5d", "h0d", "n3d", "n3u", "h1d", "x4u", "x4d", "xx2u", "xx2d", "h3d",
-    "t7", "h1u", "f3d", "f3u", "xx3u", "t6", "t1", "xx5u", "xx3d", "xx5d", "h3u", "n4u", "n4d", "xx4u", "xx4d",
-    "f4u", "f4d", "t2", "t3", "p0", "t5", "p7", "p1", "t4x", "t4z", "p6", "p2", "p5", "p3", "p4",
+    "s2", "ex0u", "s1", "rim", "s3", "sh1", "rimp", "em1d", "em1u", "m1d", "m1u", "spec", "x0d", "ex0d", "x0u",
+    "sh0", "o2", "o0", "m2d", "x1u", "x1d", "m2u", "x7d", "fix", "x7u", "c0", "n1d", "n1u", "g0u", "xx0u", "g0d",
+    "xx0d", "c2", "o3", "m3d", "x2u", "g2u", "g2d", "x2d", "x6u", "m3u", "xx7d", "o1", "xx7u", "x6d", "c1", "g1d",
+    "f1d", "f1u", "n2d", "g1u", "xx1u", "c3", "n2u", "m4d", "x3d", "xx2d", "h0u", "g3u", "g3d", "m4u", "h0d", "x3u",
+    "xx2u", "x5u", "xx1d", "f2u", "f2d", "x5d", "n3u", "n3d", "x4d", "x4u", "xx6d", "h2d", "h1u", "xx6u", "f3u",
+    "xx3u", "xx3d", "f3d", "h1d", "t1", "h2u", "xx5u", "h3d", "t0", "h3u", "xx5d", "t7", "t2", "n4d", "n4u", "xx4d",
+    "xx4u", "f4u", "t6", "f4d", "t3", "t5", "p0", "p7", "t4x", "p1", "t4z", "p6", "p2", "p5", "p3", "p4x", "p4",
 )
-N_LOCAL = 9
+N_LOADS = 10
 
 
 def kernel(
     streams, residual, short, medium, skip, w_out, fwd_a, fwd_b, inv,
-    out,
-    sx, taps, med, gain, fwd_av, fwd_bv, inv_v, res, prod, query, spec, freq, wbuf, gbuf, acc,
+    result,
+    sx, taps, med, gain, fwd_av, fwd_bv, inv_v, res, prod, query, spec, freq, wbuf, gbuf, acc, out, w_rows,
     send, recv, local,
 ):
     me, y = lax.axis_index("ctx"), lax.axis_index("ch")
@@ -75,6 +75,7 @@
     loads = {}
     for i, (name, src, dst) in enumerate(
         (
+            ("w_rows", w_out, w_rows),
             ("streams", streams, sx.at[:, pl.ds(ROWS, TOK), :]),
             ("short", short.at[:, :, owned(y)], taps),
             ("w_out", w_out.at[:, owned(y)], wbuf.at[0, c, 0, 0]),
@@ -98,6 +99,7 @@
     friends = (*z_to.values(), *x_to.values(), *y_to.values(), y_far, twin, after, before)
     for friend in friends:
         pl.semaphore_signal(barrier, inc=1, device_id=friend, device_id_type=MESH)
+    loaded("w_rows")
     pl.semaphore_wait(barrier, len(friends))
 
     moves = {}
@@ -113,7 +115,7 @@
 
     for k, device in ((1, y_to["u"]), (2, y_far), (3, y_to["d"])):
         moves[f"s{k}"] = (
-            w_out.at[:, owned(ymod(y + k))], wbuf.at[0, c, 0, NY - k], device, ()
+            w_rows.at[:, owned(ymod(y + k))], wbuf.at[0, c, 0, NY - k], device, ()
         )
     moves["rim"] = (streams.at[:, pl.ds(TOK - ROWS, ROWS), :], sx.at[:, pl.ds(0, ROWS), :], after, ())
     moves["rimp"] = (prod.at[pl.ds(TOK, FILT), :], prod.at[pl.ds(0, FILT), :], after, ("sh1",))
@@ -138,7 +140,7 @@
     from_z = {0: begun, 4: ("m4u", "m4d")}
     for way in "ud":
         near_slot = 2 if way == "u" else 1
-        mine = w_out.at[:, owned(y)]
+        mine = w_rows.at[:, owned(y)]
         moves["em1" + way] = (mine, wbuf.at[7 if way == "u" else 1, c, 0, 0], z_to[way], ())
         along_z("m1" + way, 1, way, own, rest, whole, spread)
         moves["ex0" + way] = (mine, wbuf.at[0, c, near_slot, 0], x_to[way], ())
@@ -254,16 +256,14 @@
         for part in range(BLK // 128):
             gbuf[0, b * (BLK // 128) + part] = gated[:, part * 128 : (part + 1) * 128]
 
-    projected = []
-
-    def project(dz):
+    stores = []
+
+    def project(dz, blocks):
         loaded("residual")
-        begin, end = not projected, len(projected) == NZ - 1
-        projected.append(dz)
+        begin, end = dz == 0, dz == NZ // 2
         plane = lax.rem(z + dz, NZ)
-
         left = jnp.concatenate([gbuf[g, plane] for g in range(NY)], axis=1)
-        for n in range(CH // BLK):
+        for n in blocks:
             cols = pl.ds(n * BLK, BLK)
             pieces = []
             for g in range(NY):
@@ -276,6 +276,9 @@
             total = total + jnp.dot(left, right, preferred_element_type=jnp.float32)
             if end:
                 out[:, cols] = total.astype(jnp.bfloat16)
+                store = pltpu.make_async_copy(out.at[:, cols], result.at[:, cols], local.at[N_LOADS + n])
+                store.start()
+                stores.append(store)
             else:
                 acc[:, cols] = total
 
@@ -289,9 +292,16 @@
         tasks[f"o{b}"] = (functools.partial(own_spectrum, b), ("sh1", "sh0"))
         tasks[f"c{b}"] = (functools.partial(conv_block, b), ("rimp", "fix", "spec", f"o{b}"))
     gated_all = tuple(f"{kind}{b}{way}" for kind in "gh" for b in range(CH // BLK) for way in "ud")
+    count = CH // BLK
+    others = tuple(f"p{dz}" for dz in range(NZ) if dz != NZ // 2)
     for dz in range(NZ):
-        twins = (f"t{dz}",) if dz != NZ // 2 else ("t4x", "t4z")
-        tasks[f"p{dz}"] = (functools.partial(project, dz), twins + gated_all)
+        if dz == NZ // 2:
+            early = CUT // BLK
+            tasks["p4x"] = (functools.partial(project, dz, range(early)), ("t4x",) + others)
+            tasks["p4"] = (functools.partial(project, dz, range(early, count)), ("t4x", "t4z") + others)
+        else:
+            needs = (f"t{dz}",) + (("p0",) if dz else gated_all)
+            tasks[f"p{dz}"] = (functools.partial(project, dz, range(count)), needs)
 
     copies, seen, ran = {}, set(), set()
 
@@ -325,6 +335,8 @@
             device_id_type=MESH,
         )
         copies[name].start()
+    for store in stores:
+        store.wait()
     await_all(copies)
     for copy in copies.values():
         copy.wait_send()
@@ -341,7 +353,7 @@
         kernel,
         out_shape=jax.ShapeDtypeStruct((TOK, CH), bf16),
         in_specs=[hbm] * 9,
-        out_specs=pl.BlockSpec(memory_space=pltpu.VMEM),
+        out_specs=hbm,
         scratch_shapes=[
             pltpu.VMEM((3, ROWS + TOK, CH), bf16),
             pltpu.VMEM((3, SHORT, CH), f32),
@@ -358,12 +370,14 @@
             pltpu.VMEM((NZ, NC, NX, NY, ROWS, CH), bf16),
             pltpu.VMEM((NY, CH // 128, TOK, 128), bf16),
             pltpu.VMEM((TOK, CH), f32),
+            pltpu.VMEM((TOK, CH), bf16),
+            pltpu.VMEM((ROWS, NY * CH), bf16),
             pltpu.SemaphoreType.DMA((N_COPIES,)),
             pltpu.SemaphoreType.DMA((N_COPIES,)),
-            pltpu.SemaphoreType.DMA((N_LOCAL,)),
+            pltpu.SemaphoreType.DMA((N_LOADS + CH // BLK,)),
         ],
         compiler_params=pltpu.CompilerParams(
-            collective_id=0, has_side_effects=True, vmem_limit_bytes=63 * 1024 * 1024
+            collective_id=0, has_side_effects=True, vmem_limit_bytes=60 * 1024 * 1024
         ),
     )(streams, residual_in, short_filter, medium_filter, skip_gain.reshape(1, CH), w_out, fwd_a, fwd_b, inv)
 

time: 49.6 us -> 49 us (0.988)
  Pallas kernels: 47.6 us -> 47.1 us
    pallas_call x1, Pallas kernels: 47.6 us -> 47.1 us  [on_device(): pl.pallas_call(kernel, out_shape=jax.ShapeDtypeStruct((TOK, CH), bf16), i...]
where the time goes in v2:
time: 49 us; the launch traced here: 48.9 us
  Pallas kernels  47.1 us (96%)
  local copies, waits for them, and re-layouts  1.87 us (4%)
    pallas_call x1, Pallas kernels, on_device(): pl.pallas_call(kernel, out_shape=jax.ShapeDtypeStruct((TOK, CH), bf16), i...  47.1 us
    unnamed x1, local copies, waits for them, and re-layouts  1.87 us

profile of v2, /device:TPU:1, one launch (start us, length us, event | category | flops | bytes accessed | tf_op | source)
XLA Modules:
  0.0 48.9 jit_solution(5789538698512507750)
XLA Ops:
  0.0 47.1 %shard_map.91 = bf16[256,1024]{1,0:T(8,128)(2,1)} custom-call(bf16[3,256,1024]{2,1,0:T(8,128)(2,1)} %streams.1, bf16[256,1024]{1,0:T(8,128)(2,1)} %residual.1, f32[3,7,4096]{2,1,0:T(8,128)} %short.1, bf16[128,1024]{1,0:T(8,128)(2,1)} %medium.1, f32[1,1024]{1,0:T(1,128)} %bitcast.1, bf16[16,4096]{1,0:T(8,128)(2,1)} %w_out.1, ...), custom_call_target="tpu_custom_call" | custom-call | tf_op jit(solution)/shard_map/pallas_call | solution.py:352
  47.1 1.9 %copy.11 = bf16[256,1024]{1,0:T(8,128)(2,1)} copy(bf16[256,1024]{1,0:T(8,128)(2,1)} %shard_map.91) | data formatting | bytes 1048576

commit v3 on v2

--- a/solution.py
+++ b/solution.py
@@ -34,13 +34,14 @@
 
 
 ORDER = (
-    "s2", "ex0u", "s1", "rim", "s3", "sh1", "rimp", "em1d", "em1u", "m1d", "m1u", "spec", "x0d", "ex0d", "x0u",
-    "sh0", "o2", "o0", "m2d", "x1u", "x1d", "m2u", "x7d", "fix", "x7u", "c0", "n1d", "n1u", "g0u", "xx0u", "g0d",
-    "xx0d", "c2", "o3", "m3d", "x2u", "g2u", "g2d", "x2d", "x6u", "m3u", "xx7d", "o1", "xx7u", "x6d", "c1", "g1d",
-    "f1d", "f1u", "n2d", "g1u", "xx1u", "c3", "n2u", "m4d", "x3d", "xx2d", "h0u", "g3u", "g3d", "m4u", "h0d", "x3u",
-    "xx2u", "x5u", "xx1d", "f2u", "f2d", "x5d", "n3u", "n3d", "x4d", "x4u", "xx6d", "h2d", "h1u", "xx6u", "f3u",
-    "xx3u", "xx3d", "f3d", "h1d", "t1", "h2u", "xx5u", "h3d", "t0", "h3u", "xx5d", "t7", "t2", "n4d", "n4u", "xx4d",
-    "xx4u", "f4u", "t6", "f4d", "t3", "t5", "p0", "p7", "t4x", "p1", "t4z", "p6", "p2", "p5", "p3", "p4x", "p4",
+    "s2", "s1", "ex0u", "em1d", "s3", "em1u", "rim", "sh1", "rimp", "x0d", "m1u", "m1d", "ex0d", "spec", "sh0",
+    "x0u", "fix", "o1", "o0", "x1d", "m2d", "x1u", "m2u", "xx0d", "o2", "c0", "xx0u", "x7u", "n1u", "x7d", "g0u",
+    "n1d", "g0d", "c2", "x2d", "g2d", "xx1u", "m3d", "xx1d", "g2u", "x6u", "m3u", "x6d", "x2u", "c1", "f1d", "f1u",
+    "xx7d", "o3", "c3", "g3d", "n2d", "g1u", "g3u", "n2u", "x3u", "t0", "h0u", "x5d", "m4d", "g1d", "m4u", "x3d",
+    "xx7u", "f2u", "xx6d", "xx2d", "x5u", "f2d", "h2d", "n3d", "h0d", "xx6u", "n3u", "h2u", "x4u", "t7", "x4d",
+    "f3d", "xx3u", "f3u", "xx2u", "xx3d", "h1u", "h3d", "n4d", "xx5d", "h3u", "xx5u", "h1d", "t6", "t1", "n4u",
+    "xx4u", "xx4d", "f4d", "f4u", "t3", "t2", "t5", "p0", "t4x", "p7", "t4z", "p1", "p6", "p2", "p5", "p3", "p4x",
+    "p4",
 )
 N_LOADS = 10
 

time: 49 us -> 48.7 us (level)
  no operation moved by 1% of the time
where the time goes in v3:
time: 48.7 us; the launch traced here: 48.5 us
  Pallas kernels  46.7 us (96%)
  local copies, waits for them, and re-layouts  1.87 us (4%)
    pallas_call x1, Pallas kernels, on_device(): pl.pallas_call(kernel, out_shape=jax.ShapeDtypeStruct((TOK, CH), bf16), i...  46.7 us
    unnamed x1, local copies, waits for them, and re-layouts  1.87 us

profile of v3, /device:TPU:1, one launch (start us, length us, event | category | flops | bytes accessed | tf_op | source)
XLA Modules:
  0.0 48.5 jit_solution(11766898408958902921)
XLA Ops:
  0.0 46.7 %shard_map.91 = bf16[256,1024]{1,0:T(8,128)(2,1)} custom-call(bf16[3,256,1024]{2,1,0:T(8,128)(2,1)} %streams.1, bf16[256,1024]{1,0:T(8,128)(2,1)} %residual.1, f32[3,7,4096]{2,1,0:T(8,128)} %short.1, bf16[128,1024]{1,0:T(8,128)(2,1)} %medium.1, f32[1,1024]{1,0:T(1,128)} %bitcast.1, bf16[16,4096]{1,0:T(8,128)(2,1)} %w_out.1, ...), custom_call_target="tpu_custom_call" | custom-call | tf_op jit(solution)/shard_map/pallas_call | solution.py:353
  46.7 1.9 %copy.11 = bf16[256,1024]{1,0:T(8,128)(2,1)} copy(bf16[256,1024]{1,0:T(8,128)(2,1)} %shard_map.91) | data formatting | bytes 1048576

commit v4 on v3

--- a/solution.py
+++ b/solution.py
@@ -188,7 +188,7 @@
 
     def short_rows(start, rows):
         def lane_block(b, carry):
-            lanes = pl.ds(pl.multiple_of(b * 128, 128), 128)
+            lanes = pl.ds(pl.multiple_of(b * BLK, BLK), BLK)
             done = []
             for s in range(3):
                 window = sx[s, pl.ds(start, rows + ROWS), lanes].astype(jnp.float32)
@@ -201,7 +201,7 @@
             prod[pl.ds(FILT + start, rows), lanes] = (done[1] * done[2]).astype(jnp.bfloat16)
             return carry
 
-        lax.fori_loop(0, CH // 128, lane_block, 0)
+        lax.fori_loop(0, CH // BLK, lane_block, 0)
 
     def short_last():
         loaded("streams", "short")

time: 48.7 us -> 48.6 us (level)
  no operation moved by 1% of the time
where the time goes in v4:
time: 48.6 us; the launch traced here: 48.5 us
  Pallas kernels  46.6 us (96%)
  local copies, waits for them, and re-layouts  1.87 us (4%)
    pallas_call x1, Pallas kernels, on_device(): pl.pallas_call(kernel, out_shape=jax.ShapeDtypeStruct((TOK, CH), bf16), i...  46.6 us
    unnamed x1, local copies, waits for them, and re-layouts  1.87 us

profile of v4, /device:TPU:1, one launch (start us, length us, event | category | flops | bytes accessed | tf_op | source)
XLA Modules:
  0.0 48.5 jit_solution(16457258179214351486)
XLA Ops:
  0.0 46.6 %shard_map.91 = bf16[256,1024]{1,0:T(8,128)(2,1)} custom-call(bf16[3,256,1024]{2,1,0:T(8,128)(2,1)} %streams.1, bf16[256,1024]{1,0:T(8,128)(2,1)} %residual.1, f32[3,7,4096]{2,1,0:T(8,128)} %short.1, bf16[128,1024]{1,0:T(8,128)(2,1)} %medium.1, f32[1,1024]{1,0:T(1,128)} %bitcast.1, bf16[16,4096]{1,0:T(8,128)(2,1)} %w_out.1, ...), custom_call_target="tpu_custom_call" | custom-call | tf_op jit(solution)/shard_map/pallas_call | solution.py:353
  46.6 1.9 %copy.11 = bf16[256,1024]{1,0:T(8,128)(2,1)} copy(bf16[256,1024]{1,0:T(8,128)(2,1)} %shard_map.91) | data formatting | bytes 1048576
